TPU v7x, 32 devices: a whole 2x2x4 slice. The times are simulated.
32 devices in a mesh: batch: 16 (over z, y, x), mp: 2 (over core).
Axes of the slice: x: 2, y: 2, z: 4, core: 2. Of those that a mesh axis runs over, the one named last changes fastest.
Arguments:
- hidden_in: bfloat16 [32, 1024, 768], P('batch', 'mp'), may hold values from -6 to 6
- memory_flags: int32 [32], P('batch'), may hold values 0 or 1
- memory_coeffs: bfloat16 [32, 256, 768], P('batch', 'mp'), may hold values from -6 to 6
- first_gain: float32 [768], replicated, may hold values from 0.25 to 1.75
- first_bias: float32 [768], replicated, may hold values from -1.5 to 1.5
- query_key_value_matrix: bfloat16 [768, 3, 768], P(None, None, 'mp'), may hold values from -0.21875 to 0.21875
- qv_bias: bfloat16 [2, 768], P(None, 'mp'), may hold values from -1.5 to 1.5
- memory_weight: bfloat16 [2, 12, 256], P(None, 'mp'), may hold values from -0.1875 to 0.1875
- memory_bias: bfloat16 [2, 12], P(None, 'mp'), may hold values from -1.5 to 1.5
- output_matrix: bfloat16 [768, 768], P('mp'), may hold values from -1.25 to 1.25
- out_bias: float32 [768], replicated, may hold values from -1.5 to 1.5
- second_gain: float32 [768], replicated, may hold values from 0.25 to 1.75
- second_bias: float32 [768], replicated, may hold values from -1.5 to 1.5
- up_matrix: bfloat16 [768, 3072], P(None, 'mp'), may hold values from -0.21875 to 0.21875
- up_bias_vector: bfloat16 [3072], P('mp'), may hold values from -1.5 to 1.5
- down_matrix: bfloat16 [3072, 768], P('mp'), may hold values from -0.109375 to 0.109375
- down_bias: float32 [768], replicated, may hold values from -1.5 to 1.5
- out_grad: bfloat16 [32, 1024, 768], P('batch', 'mp'), may hold values from -6 to 6
Outputs:
- block_out: bfloat16 [32, 1024, 768], P('batch', 'mp')
- input_grad: float32 [32, 1024, 768], P('batch', 'mp')
- coeff_grad: float32 [32, 256, 768], P('batch', 'mp')
- first_gain_grad: float32 [768], replicated
- first_bias_grad: float32 [768], replicated
- query_key_value_matrix_grad: float32 [768, 3, 768], P(None, None, 'mp')
- qv_bias_grad: float32 [2, 768], P(None, 'mp')
- memory_weight_grad: float32 [2, 12, 256], P(None, 'mp')
- memory_bias_grad: float32 [2, 12], P(None, 'mp')
- output_matrix_grad: float32 [768, 768], P('mp')
- out_bias_grad: float32 [768], replicated
- second_gain_grad: float32 [768], replicated
- second_bias_grad: float32 [768], replicated
- up_weight_grad: float32 [768, 3072], P(None, 'mp')
- up_bias_grad: float32 [3072], P('mp')
- down_weight_grad: float32 [3072, 768], P('mp')
- down_bias_grad: float32 [768], replicated
Inputs may be any that keep to these rules, and one draw needn't show every extreme that they name: memory_flags holds one flag per sequence.
All inputs are finite; a program needn't handle non-finite values. No bound on the sum of `memory_flags` on one device may be relied on, other than what follows from the above.
Results may differ from a plain program's by a relative error of at most 0.013.
The roundings to bfloat16 on the way count: a program that leaves them out, or rounds other values in their place, can miss the bound.
Values may be sent and summed in bfloat16 or wider, within the bound.
No kernel may reach another device: no remote copies, remote signals or barrier semaphores. Data moves between devices by JAX's collectives and lax.ppermute only.
A program may use at most 320 MiB of HBM per device.

v0:
```python
import math
import jax
import jax.numpy as jnp
from jax import lax
from jax.sharding import PartitionSpec as P

HD = 64


def product(form, left_side, right_side):
    return jnp.einsum(form, left_side, right_side, precision=lax.Precision.HIGHEST)


def matrix_multiply(form, left_side, right_side):
    return jnp.einsum(form, left_side, right_side, preferred_element_type=jnp.float32)


def norm_parts(values, gain_vec, bias_vec):
    row_mean = jnp.mean(values, axis=-1, keepdims=True)
    centred = values - row_mean
    row_var = jnp.mean(centred * centred, axis=-1, keepdims=True)
    inverse = lax.rsqrt(row_var + 1e-05)
    scaled = centred * inverse
    return (scaled * gain_vec + bias_vec, scaled, inverse)


def norm_back(grad_out, scaled, inverse, gain_vec):
    grad_scaled = grad_out * gain_vec
    first_mean = jnp.mean(grad_scaled, axis=-1, keepdims=True)
    second_mean = jnp.mean(grad_scaled * scaled, axis=-1, keepdims=True)
    return inverse * (grad_scaled - first_mean - scaled * second_mean)


def basis_weights(memory_scores, weight_pair, bias_pair):
    basis_count = memory_scores.shape[-1]
    mean_logit = product("slhn,hn->slh", memory_scores, weight_pair[0]) + bias_pair[0]
    var_logit = product("slhn,hn->slh", memory_scores, weight_pair[1]) + bias_pair[1]
    centre = jax.nn.sigmoid(mean_logit)
    spread = 0.05 * jax.nn.softplus(var_logit) + (8.0 / basis_count) ** 2
    places = (jnp.arange(basis_count, dtype=jnp.float32) + 0.5) / basis_count
    offset = places - centre[..., None]
    return (
        jnp.exp(-offset * offset / (2.0 * spread[..., None]))
        * lax.rsqrt(2.0 * math.pi * spread[..., None])
        / basis_count
    )


def causal_scores(block_queries, key_rows, start_row, end_row):
    scores = matrix_multiply("sqhd,skhd->shqk", block_queries, key_rows[:, :end_row]) * 0.125
    allowed = jnp.arange(end_row)[None, :] <= jnp.arange(start_row, end_row)[:, None]
    return jnp.where(allowed, scores, -1e30)


def attend_forward(
    norm_output,
    coeffs,
    flag_vec,
    query_key_value_matrix,
    qv_bias,
    memory_weight,
    memory_bias,
    output_matrix,
):
    seq_count, length, model_width = norm_output.shape
    local_width = query_key_value_matrix.shape[2]
    head_count = local_width // HD
    basis_count = coeffs.shape[1]
    head_shape = (seq_count, length, head_count, HD)
    bias_values = qv_bias.astype(jnp.float32)
    projected_rows = matrix_multiply("zam,mwr->zawr", norm_output, query_key_value_matrix)
    queries = (projected_rows[:, :, 0] + bias_values[0]).astype(jnp.bfloat16).reshape(head_shape)
    key_rows = projected_rows[:, :, 1].astype(jnp.bfloat16).reshape(head_shape)
    values = (projected_rows[:, :, 2] + bias_values[1]).astype(jnp.bfloat16).reshape(head_shape)
    memory = matrix_multiply("snd,dcf->sncf", coeffs, query_key_value_matrix[:, 1:]).astype(
        jnp.bfloat16
    )
    memory_keys = memory[:, :, 0].reshape(seq_count, basis_count, head_count, HD)
    memory_values = memory[:, :, 1].reshape(seq_count, basis_count, head_count, HD)
    block_rows = min(512, length)
    attended_parts = []
    total_parts = []
    for block_index in range(length // block_rows):
        start_row = block_index * block_rows
        end_row = start_row + block_rows
        scores = causal_scores(queries[:, start_row:end_row], key_rows, start_row, end_row)
        top_score = jnp.max(scores, axis=-1, keepdims=True)
        raised = jnp.exp(scores - top_score)
        denominator = jnp.sum(raised, axis=-1, keepdims=True)
        weights = (raised / denominator).astype(jnp.bfloat16)
        attended_parts.append(matrix_multiply("shqk,skhd->sqhd", weights, values[:, :end_row]))
        total_parts.append(top_score[..., 0] + jnp.log(denominator[..., 0]))
    attended = jnp.concatenate(attended_parts, axis=1)
    log_totals = jnp.concatenate(total_parts, axis=2)
    memory_scores = matrix_multiply("slhd,snhd->slhn", queries, memory_keys) * 0.125
    basis_mass = basis_weights(
        memory_scores, memory_weight.astype(jnp.float32), memory_bias.astype(jnp.float32)
    ).astype(jnp.bfloat16)
    recalled = matrix_multiply("slhn,snhd->slhd", basis_mass, memory_values)
    flag_values = flag_vec.astype(jnp.float32)[:, None, None, None]
    combined_heads = (
        (attended + flag_values * recalled)
        .astype(jnp.bfloat16)
        .reshape(seq_count, length, local_width)
    )
    residual_piece = matrix_multiply("hom,mu->hou", combined_heads, output_matrix)
    kept = (
        queries,
        key_rows,
        values,
        memory_keys,
        memory_values,
        memory_scores,
        basis_mass,
        combined_heads,
        log_totals,
    )
    return (residual_piece, kept)


def attend_backward(
    residual_grad,
    norm_output,
    coeffs,
    flag_vec,
    query_key_value_matrix,
    memory_weight,
    memory_bias,
    output_matrix,
    kept,
):
    (
        queries,
        key_rows,
        values,
        memory_keys,
        memory_values,
        memory_scores,
        basis_mass,
        combined_heads,
        log_totals,
    ) = kept
    seq_count, length, model_width = norm_output.shape
    local_width = query_key_value_matrix.shape[2]
    head_count = local_width // HD
    basis_count = coeffs.shape[1]
    output_matrix_grad = matrix_multiply("qro,qrv->ov", combined_heads, residual_grad)
    combined_heads_grad = matrix_multiply("kpo,wo->kpw", residual_grad, output_matrix).astype(
        jnp.bfloat16
    )
    combined_heads_grad = combined_heads_grad.reshape(seq_count, length, head_count, HD)
    recalled_grad = combined_heads_grad * flag_vec[:, None, None, None]
    basis_grad = matrix_multiply("slhd,snhd->slhn", recalled_grad, memory_values)
    mvalues_grad = matrix_multiply("slhn,slhd->snhd", basis_mass, recalled_grad)
    unused_mass, pullback = jax.vjp(
        basis_weights,
        memory_scores,
        memory_weight.astype(jnp.float32),
        memory_bias.astype(jnp.float32),
    )
    scores_grad, memory_weight_grad, memory_bias_grad = pullback(basis_grad)
    scores_grad = scores_grad.astype(jnp.bfloat16)
    query_grad = matrix_multiply("slhn,snhd->slhd", scores_grad, memory_keys) * 0.125
    mkeys_grad = matrix_multiply("slhn,slhd->snhd", scores_grad, queries) * 0.125
    key_grad = jnp.zeros(key_rows.shape, jnp.float32)
    value_grad = jnp.zeros(values.shape, jnp.float32)
    block_rows = min(512, length)
    query_parts = []
    for block_index in range(length // block_rows):
        start_row = block_index * block_rows
        end_row = start_row + block_rows
        block_queries = queries[:, start_row:end_row]
        block_grad = combined_heads_grad[:, start_row:end_row]
        scores = causal_scores(block_queries, key_rows, start_row, end_row)
        weights = jnp.exp(scores - log_totals[:, :, start_row:end_row, None])
        weights_grad = matrix_multiply("sqhd,skhd->shqk", block_grad, values[:, :end_row])
        inner_sum = jnp.sum(weights * weights_grad, axis=-1, keepdims=True)
        block_scores_grad = (weights * (weights_grad - inner_sum)).astype(jnp.bfloat16)
        query_parts.append(
            matrix_multiply("shqk,skhd->sqhd", block_scores_grad, key_rows[:, :end_row]) * 0.125
        )
        key_grad = key_grad.at[:, :end_row].add(
            matrix_multiply("shqk,sqhd->skhd", block_scores_grad, block_queries) * 0.125
        )
        value_grad = value_grad.at[:, :end_row].add(
            matrix_multiply("shqk,sqhd->skhd", weights.astype(jnp.bfloat16), block_grad)
        )
    query_grad = query_grad + jnp.concatenate(query_parts, axis=1)
    query_key_value_rows_grad = jnp.stack([query_grad, key_grad, value_grad], axis=2).astype(
        jnp.bfloat16
    )
    query_key_value_rows_grad = query_key_value_rows_grad.reshape(seq_count, length, 3, local_width)
    memory_grads = jnp.stack([mkeys_grad, mvalues_grad], axis=2).astype(jnp.bfloat16)
    memory_grads = memory_grads.reshape(seq_count, basis_count, 2, local_width)
    query_key_value_matrix_grad = matrix_multiply(
        "arh,arkq->hkq", norm_output, query_key_value_rows_grad
    )
    query_key_value_matrix_grad = query_key_value_matrix_grad.at[:, 1:].add(
        matrix_multiply("snd,sncf->dcf", coeffs, memory_grads)
    )
    qv_bias_grad = jnp.sum(query_key_value_rows_grad[:, :, 0::2].astype(jnp.float32), axis=(0, 1))
    norm_output_grad = matrix_multiply(
        "zwev,oev->zwo", query_key_value_rows_grad, query_key_value_matrix
    )
    coeffs_grad = matrix_multiply("sncf,dcf->snd", memory_grads, query_key_value_matrix[:, 1:])
    return (
        norm_output_grad,
        coeffs_grad,
        query_key_value_matrix_grad,
        qv_bias_grad,
        memory_weight_grad,
        memory_bias_grad,
        output_matrix_grad,
    )


def feed_forward(norm_output, up_matrix, up_bias_vector, down_matrix):
    input_rows = matrix_multiply("ahg,gm->ahm", norm_output, up_matrix) + up_bias_vector.astype(
        jnp.float32
    )
    gelu_output = jax.nn.gelu(input_rows, approximate=True).astype(jnp.bfloat16)
    return (matrix_multiply("hom,mu->hou", gelu_output, down_matrix), input_rows, gelu_output)


def feed_backward(gradient_rows, norm_output, up_matrix, down_matrix, input_rows, gelu_output):
    down_output_grad = matrix_multiply("qro,qrv->ov", gelu_output, gradient_rows)
    hidden_state_grad = matrix_multiply("kpo,wo->kpw", gradient_rows, down_matrix)
    unused_value, pullback = jax.vjp(
        lambda inputs: jax.nn.gelu(inputs, approximate=True), input_rows
    )
    (input_rows_grad,) = pullback(hidden_state_grad)
    input_rows_grad = input_rows_grad.astype(jnp.bfloat16)
    up_output_grad = matrix_multiply("orx,ora->xa", norm_output, input_rows_grad)
    upb_grad = jnp.sum(input_rows_grad.astype(jnp.float32), axis=(0, 1))
    norm_output_grad = matrix_multiply("iqg,kg->iqk", input_rows_grad, up_matrix)
    return (norm_output_grad, up_output_grad, upb_grad, down_output_grad)


def per_device(
    hidden_in,
    memory_flags,
    memory_coeffs,
    first_gain,
    first_bias,
    query_key_value_matrix,
    qv_bias,
    memory_weight,
    memory_bias,
    output_matrix,
    out_bias,
    second_gain,
    second_bias,
    up_matrix,
    up_bias_vector,
    down_matrix,
    down_bias,
    out_grad,
):
    hidden = hidden_in.astype(jnp.float32)
    flag_local = memory_flags.astype(jnp.bfloat16)
    normed_one, scaled_one, inverse_one = norm_parts(hidden, first_gain, first_bias)
    normed_one = normed_one.astype(jnp.bfloat16)
    normed_all, coeffs_all = (
        lax.all_gather(normed_one, "mp", axis=1, tiled=True),
        lax.all_gather(memory_coeffs, "mp", axis=1, tiled=True),
    )
    residual_piece, kept = attend_forward(
        normed_all,
        coeffs_all,
        flag_local,
        query_key_value_matrix,
        qv_bias,
        memory_weight,
        memory_bias,
        output_matrix,
    )
    branch_total = lax.psum_scatter(residual_piece, "mp", scatter_dimension=1, tiled=True)
    middle = hidden + (branch_total + out_bias)
    normed_two, scaled_two, inverse_two = norm_parts(middle, second_gain, second_bias)
    normed_two_all = lax.all_gather(normed_two.astype(jnp.bfloat16), "mp", axis=1, tiled=True)
    feed_part, input_rows, gelu_output = feed_forward(
        normed_two_all, up_matrix, up_bias_vector, down_matrix
    )
    feed_total = lax.psum_scatter(
        feed_part.astype(jnp.bfloat16), "mp", scatter_dimension=1, tiled=True
    ).astype(jnp.float32)
    block_out = (middle + feed_total + down_bias).astype(jnp.bfloat16)
    grad_all = lax.all_gather(out_grad, "mp", axis=1, tiled=True)
    normed_two_part, up_output_grad, upb_grad, down_output_grad = feed_backward(
        grad_all, normed_two_all, up_matrix, down_matrix, input_rows, gelu_output
    )
    normed_two_grad = lax.psum_scatter(normed_two_part, "mp", scatter_dimension=1, tiled=True)
    out_grad_values = out_grad.astype(jnp.float32)
    middle_grad = out_grad_values + norm_back(normed_two_grad, scaled_two, inverse_two, second_gain)
    second_gain_grad = jnp.sum(normed_two_grad * scaled_two, axis=(0, 1))
    second_bias_grad = jnp.sum(normed_two_grad, axis=(0, 1))
    down_bias_grad = jnp.sum(out_grad_values, axis=(0, 1))
    residual_grad = middle_grad.astype(jnp.bfloat16)
    out_bias_grad = jnp.sum(residual_grad.astype(jnp.float32), axis=(0, 1))
    branch_grad_all = lax.all_gather(residual_grad, "mp", axis=1, tiled=True)
    normed_part, coeffs_part, qkv_grad, qv_grad, memw_grad, memb_grad, outw_grad = attend_backward(
        branch_grad_all,
        normed_all,
        coeffs_all,
        flag_local,
        query_key_value_matrix,
        memory_weight,
        memory_bias,
        output_matrix,
        kept,
    )
    normed_one_grad, coeff_grad = (
        lax.psum_scatter(
            normed_part.astype(jnp.bfloat16), "mp", scatter_dimension=1, tiled=True
        ).astype(jnp.float32),
        lax.psum_scatter(
            coeffs_part.astype(jnp.bfloat16), "mp", scatter_dimension=1, tiled=True
        ).astype(jnp.float32),
    )
    input_grad = middle_grad + norm_back(normed_one_grad, scaled_one, inverse_one, first_gain)
    first_gain_grad = jnp.sum(normed_one_grad * scaled_one, axis=(0, 1))
    first_bias_grad = jnp.sum(normed_one_grad, axis=(0, 1))
    (
        qkv_grad,
        qv_grad,
        memw_grad,
        memb_grad,
        outw_grad,
        up_output_grad,
        upb_grad,
        down_output_grad,
    ) = lax.psum(
        (
            qkv_grad,
            qv_grad,
            memw_grad,
            memb_grad,
            outw_grad,
            up_output_grad,
            upb_grad,
            down_output_grad,
        ),
        "batch",
    )
    (
        first_gain_grad,
        first_bias_grad,
        out_bias_grad,
        second_gain_grad,
        second_bias_grad,
        down_bias_grad,
    ) = lax.psum(
        (
            first_gain_grad,
            first_bias_grad,
            out_bias_grad,
            second_gain_grad,
            second_bias_grad,
            down_bias_grad,
        ),
        ("batch", "mp"),
    )
    return (
        block_out,
        input_grad,
        coeff_grad,
        first_gain_grad,
        first_bias_grad,
        qkv_grad,
        qv_grad,
        memw_grad,
        memb_grad,
        outw_grad,
        out_bias_grad,
        second_gain_grad,
        second_bias_grad,
        up_output_grad,
        upb_grad,
        down_output_grad,
        down_bias_grad,
    )


def solution(mesh):
    placed = (
        P("batch", "mp", None),
        P("batch"),
        P("batch", "mp", None),
        P(),
        P(),
        P(None, None, "mp"),
        P(None, "mp"),
        P(None, "mp", None),
        P(None, "mp"),
        P("mp", None),
        P(),
        P(),
        P(),
        P(None, "mp"),
        P("mp"),
        P("mp", None),
        P(),
        P("batch", "mp", None),
    )
    return jax.shard_map(
        per_device,
        mesh=mesh,
        in_specs=placed,
        out_specs=(
            P("batch", "mp", None),
            P("batch", "mp", None),
            P("batch", "mp", None),
            P(),
            P(),
            P(None, None, "mp"),
            P(None, "mp"),
            P(None, "mp", None),
            P(None, "mp"),
            P("mp", None),
            P(),
            P(),
            P(),
            P(None, "mp"),
            P("mp"),
            P("mp", None),
            P(),
        ),
        check_vma=False,
    )
```

profile of v0, /device:TPU:0, one launch (start us, length us, event | category | flops | bytes accessed | tf_op | source)
XLA Modules:
  0.0 850.8 jit_solution(11959987445198987662)
XLA Ops:
  50.0 7.1 fusion.54
  57.1 10.7 %fusion.34 = (f32[2,6,512]{2,1,0:T(8,128)S(1)}, f32[2,6,512,1024]{3,2,1,0:T(8,128)}) fusion(pred[512,1024]{1,0:T(8,128)(4,1)S(1)} %iota_compare_fusion, bf16[2,1024,6,64]{1,3,2,0:T(8,128)(2,1)S(1)} %bitcast.292, bf16[2,1024,6,64]{1,3,2,0:T(8,128)(2,1)S(1)} %add_convert_fusion.3), kind=kOutput, calls=%fused_computation.57 | convolution fusion | flops 824174592 | bytes 28073984 | tf_op jit(solution)/shard_map/sqhd,skhd->shqk/dot_general | solution.py:15
  68.1 7.7 fusion.24
  75.9 7.7 fusion.98
  85.9 7.3 fusion
  93.3 8.5 %fusion.102 = f32[2,512,6,64]{1,3,2,0:T(8,128)} fusion(bf16[2,1024,6,64]{1,3,2,0:T(8,128)(2,1)S(1)} %add_convert_fusion.4, f32[2,6,512]{2,1,0:T(8,128)S(1)} %fusion, f32[2,6,512]{2,1,0:T(8,128)S(1)} %get-tuple-element.164, f32[2,6,512,1024]{3,2,1,0:T(8,128)S(1)} %bitcast.288, pred[512,1024]{1,0:T(8,128)(4,1)S(1)} %iota_compare_fusion), kind=kOutput, calls=%fused_computation.147 | convolution fusion | flops 836763648 | bytes 28884992 | tf_op jit(solution)/shard_map/shqk,skhd->sqhd/dot_general | solution.py:15
  102.8 16.8 %fusion.70 = bf16[2,1024,6,64]{1,3,2,0:T(8,128)(2,1)S(1)} fusion(f32[2,512,6,64]{1,3,2,0:T(8,128)} %fusion.102, f32[2,512,6,64]{1,3,2,0:T(8,128)} %fusion.98, bf16[2,256,6,64]{1,3,2,0:T(8,128)(2,1)S(1)} %bitcast.314, f32[2,1024,6]{1,2,0:T(8,128)S(1)} %get-tuple-element.149, f32[2,1024,6]{1,2,0:T(8,128)S(1)} %get-tuple-element.151, ...), kind=kOutput, calls=%fused_computation.105 | convolution fusion | flops 427819008 | bytes 5260296 | tf_op jit(solution)/shard_map/slhn,snhd->slhd/dot_general | solution.py:15
  125.3 15.8 %reduce-scatter.6.cloned.1.call-done = f32[2,512,768]{2,1,0:T(8,128)} async-done(((f32[2,1024,768]{2,1,0:T(8,128)}), f32[2,512,768]{2,1,0:T(8,128)}) %reduce-scatter.6.cloned.1.call-update) | async-done | bytes 3145744 | tf_op jit(solution)/shard_map/reduce_scatter | solution.py:277
  148.0 12.8 %all-gather.7.cloned.1.call-done = bf16[2,1024,768]{2,1,0:T(8,128)(2,1)} async-done(((bf16[2,512,768]{2,1,0:T(8,128)(2,1)}), bf16[2,1024,768]{2,1,0:T(8,128)(2,1)}) %all-gather.7.cloned.1.call-update) | async-done | bytes 3145744 | tf_op jit(solution)/shard_map/all_gather | solution.py:280
  160.8 13.4 %multiply_convert_fusion.2 = (bf16[2,1024,1536]{2,1,0:T(8,128)(2,1)}, f32[2,1024,1536]{2,1,0:T(8,128)}) fusion(f32[1536]{0:T(1024)S(1)} %convert_element_type.137, bf16[2,1024,768]{2,1,0:T(8,128)(2,1)} %all-gather.7.cloned.1.call-done, bf16[768,1536]{1,0:T(8,128)(2,1)S(1)} %copy-done), kind=kOutput, calls=%fused_computation.40 | convolution fusion | flops 4863295488 | bytes 24385536 | tf_op jit(solution)/shard_map/ahg,gm->ahm/dot_general | solution.py:15
  175.6 17.3 %convert_reduce_fusion = (f32[1536]{0:T(1024)}, bf16[2,1024,1536]{2,1,0:T(8,128)(2,1)S(1)}) fusion(f32[2,1024,1536]{2,1,0:T(8,128)} %get-tuple-element.171, f32[1536]{0:T(1024)S(1)} %convert_element_type.137, bf16[2,1024,768]{2,1,0:T(8,128)(2,1)} %all-gather.9.cloned.1.call-done, bf16[1536,768]{1,0:T(8,128)(2,1)} %param.47), kind=kOutput, calls=%fused_computation.34 | convolution fusion | flops 4904188416 | bytes 24391680 | tf_op jit(solution)/shard_map/kpo,wo->kpw/dot_general | solution.py:15
  195.6 6.9 fusion.82
  202.5 15.8 %reduce-scatter.10.cloned.1.call-done = f32[2,512,768]{2,1,0:T(8,128)} async-done(((f32[2,1024,768]{2,1,0:T(8,128)}), f32[2,512,768]{2,1,0:T(8,128)}) %reduce-scatter.10.cloned.1.call-update) | async-done | bytes 3145744 | tf_op jit(solution)/shard_map/reduce_scatter | solution.py:292
  227.5 13.3 %all-gather.11.cloned.1.call-done = bf16[2,1024,768]{2,1,0:T(8,128)(2,1)} async-done(((bf16[2,512,768]{2,1,0:T(8,128)(2,1)}), bf16[2,1024,768]{2,1,0:T(8,128)(2,1)}) %all-gather.11.cloned.1.call-update) | async-done | bytes 3145744 | tf_op jit(solution)/shard_map/all_gather | solution.py:300
  244.3 8.0 fusion.99
  259.6 7.1 multiply_convert_fusion.1
  276.7 11.3 %fusion.6 = (f32[2,1024,6]{1,2,0:T(8,128)S(1)}, f32[2,1024,6]{1,2,0:T(8,128)S(1)}, f32[2,1024,6]{1,2,0:T(8,128)S(1)}) fusion(f32[2,1024,6]{1,2,0:T(8,128)S(1)} %copy-done.52, f32[2,1024,6]{1,2,0:T(8,128)S(1)} %copy-done.58, f32[256]{0:T(256)S(1)} %copy-done.90, f32[2,1024,6]{1,2,0:T(8,128)S(1)} %copy-done.54, f32[2,1024,6]{1,2,0:T(8,128)S(1)} %get-tuple-element.148, ...), kind=kOutput, calls=%fused_computation.17 | convolution fusion | flops 460025856 | bytes 2311172 | tf_op jit(solution)/shard_map/slhd,snhd->slhn/dot_general | solution.py:15
  298.0 18.1 %multiply_reduce_fusion = (f32[2,6,512]{2,1,0:T(8,128)S(1)}, f32[2,6,512,1024]{3,2,1,0:T(8,128)}) fusion(f32[2,6,512]{2,1,0:T(8,128)S(1)} %log_add_fusion, f32[2,6,512,1024]{3,2,1,0:T(8,128)} %get-tuple-element.165, pred[512,1024]{1,0:T(8,128)(4,1)S(1)} %copy-done.8, bf16[2,1024,6,64]{1,3,2,0:T(8,128)(2,1)} %copy-done.16, bf16[2,1024,6,64]{1,3,2,0:T(8,128)(2,1)} %bitcast.312), kind=kOutput, calls=%fused_computation.1 | convolution fusion | flops 836757504 | bytes 53264384 | tf_op jit(solution)/shard_map/sqhd,skhd->shqk/dot_general | solution.py:15
  316.1 13.5 %fusion.76 = bf16[2,1024,6,64]{1,3,2,0:T(8,128)(2,1)} fusion(f32[2,512,6,64]{1,3,2,0:T(8,128)} %fusion.99, f32[2,6,512]{2,1,0:T(8,128)S(1)} %log_add_fusion, f32[2,6,512,1024]{3,2,1,0:T(8,128)} %get-tuple-element.165, pred[512,1024]{1,0:T(8,128)(4,1)S(1)} %copy-done.8, bf16[2,1024,6,64]{1,3,2,0:T(8,128)(2,1)} %bitcast.313), kind=kOutput, calls=%fused_computation.113 | convolution fusion | flops 832045056 | bytes 29646848 | tf_op jit(solution)/shard_map/shqk,sqhd->skhd/dot_general | solution.py:15
  332.1 21.4 %multiply_convert_fusion = bf16[2,6,512,1024]{3,2,1,0:T(8,128)(2,1)} fusion(f32[2,6,512,1024]{3,2,1,0:T(8,128)} %get-tuple-element.169, f32[2,6,512]{2,1,0:T(8,128)S(1)} %get-tuple-element.168, f32[2,6,512]{2,1,0:T(8,128)S(1)} %log_add_fusion, f32[2,6,512,1024]{3,2,1,0:T(8,128)} %get-tuple-element.165, pred[512,1024]{1,0:T(8,128)(4,1)S(1)} %copy-done.8), kind=kLoop, calls=%fused_computation | loop fusion | flops 37748736 | bytes 63488000 | tf_op jit(solution)/shard_map/convert_element_type | solution.py:178
  353.5 8.6 %multiply_bitcast_fusion.2 = f32[2,512,6,64]{1,3,2,0:T(8,128)S(1)} fusion(bf16[2,1024,6,64]{1,3,2,0:T(8,128)(2,1)S(1)} %bitcast.294, bf16[2,6,512,1024]{3,2,1,0:T(8,128)(2,1)} %multiply_convert_fusion), kind=kOutput, calls=%fused_computation.143 | convolution fusion | flops 805699584 | bytes 15728640 | tf_op jit(solution)/shard_map/shqk,skhd->sqhd/dot_general | solution.py:15
  370.6 8.4 fusion.77
  381.8 8.4 bitcast_convert_fusion
  390.3 9.0 %fusion.86 = bf16[2,1024,768]{2,1,0:T(8,128)(2,1)} fusion(bf16[2,1024,1536]{2,1,0:T(8,128)(2,1)} %get-tuple-element.170, bf16[1536,768]{1,0:T(8,128)(2,1)} %param.47), kind=kOutput, calls=%fused_computation.135 | convolution fusion | flops 4833411072 | bytes 11796480 | tf_op jit(solution)/shard_map/hom,mu->hou/dot_general | solution.py:15
  399.4 10.4 %convolution_bitcast_fusion.1 = f32[768,1536]{1,0:T(8,128)} fusion(bf16[2,1024,768]{2,1,0:T(8,128)(2,1)} %all-gather.7.cloned.1.call-done, bf16[2,1024,1536]{2,1,0:T(8,128)(2,1)} %copy-done.91), kind=kOutput, calls=%fused_computation.90 | convolution fusion | flops 4831838208 | bytes 14155776 | tf_op jit(solution)/shard_map/orx,ora->xa/dot_general | solution.py:15
  409.7 8.9 %convolution_bitcast_fusion = f32[1536,768]{1,0:T(8,128)} fusion(bf16[2,1024,1536]{2,1,0:T(8,128)(2,1)} %get-tuple-element.170, bf16[2,1024,768]{2,1,0:T(8,128)(2,1)S(1)} %copy-done.85), kind=kOutput, calls=%fused_computation.89 | convolution fusion | flops 4831838208 | bytes 14155776 | tf_op jit(solution)/shard_map/qro,qrv->ov/dot_general | solution.py:15
  432.0 13.3 %fusion.27 = f32[6,1,256,1]{2,1,3,0:T(1,128)S(1)} fusion(f32[2,1024,6,256]{1,3,2,0:T(8,128)} %copy-done.2, f32[6,2,1024,1]{2,0,1,3:T(8,128)S(1)} %bitcast.319), kind=kOutput, calls=%fused_computation.50 | convolution fusion | flops 37748736 | bytes 12638208 | tf_op jit(solution)/shard_map/transpose(jvp(slhn,hn->slh))/dot_general | solution.py:11
  445.4 13.4 %fusion.25 = f32[6,1,256,1]{2,1,3,0:T(1,128)S(1)} fusion(f32[2,1024,6,256]{1,3,2,0:T(8,128)} %copy-done.2, f32[6,2,1024,1]{2,0,1,3:T(8,128)S(1)} %bitcast.318), kind=kOutput, calls=%fused_computation.48 | convolution fusion | flops 37748736 | bytes 12638208 | tf_op jit(solution)/shard_map/transpose(jvp(slhn,hn->slh))/dot_general | solution.py:11
  460.5 81.6 %all-reduce.7 = (f32[2,384]{1,0:T(2,128)}, f32[2,6,256]{2,1,0:T(8,128)S(1)}, f32[2,6]{1,0:T(2,128)}, f32[1536]{0:T(1024)}) all-reduce(f32[2,384]{1,0:T(2,128)S(1)} %convert_reduce_fusion.1, f32[2,6,256]{2,1,0:T(8,128)S(1)} %pad_add_fusion, f32[2,6]{1,0:T(2,128)S(1)} %pad_add_fusion.1, ...), channel_id=1, replica_groups=mesh['batch'=16,'mp'=2] {'batch'}, use_global_device_ids=true, to_apply=%region_28.29 | all-reduce | flops 5388 | bytes 43104 | tf_op jit(solution)/shard_map/psum | solution.py:332
  547.7 8.3 fusion.66
  556.0 40.4 %all-reduce.6 = (f32[768]{0:T(1024)}, f32[768]{0:T(1024)}, f32[768]{0:T(1024)}, f32[768]{0:T(1024)}, f32[768]{0:T(1024)}, /*index=5*/f32[768]{0:T(1024)}) all-reduce(f32[768]{0:T(1024)S(1)} %get-tuple-element.115, f32[768]{0:T(1024)S(1)} %get-tuple-element.120, ...), channel_id=1, replica_groups=mesh['batch'=16,'mp'=2] {'batch','mp'}, use_global_device_ids=true, to_apply=%region_23.24 | all-reduce | flops 4608 | bytes 36864 | tf_op jit(solution)/shard_map/psum | solution.py:352
  596.4 236.2 %all-reduce.11.cloned.1.call-done = (f32[768,3,384]{2,0,1:T(8,128)}, f32[384,768]{1,0:T(8,128)}, f32[768,1536]{1,0:T(8,128)}, f32[1536,768]{1,0:T(8,128)}) async-done(((f32[768,3,384]{2,0,1:T(8,128)}, f32[384,768]{1,0:T(8,128)}, f32[768,1536]{1,0:T(8,128)}, f32[1536,768]{1,0:T(8,128)}), (f32[768,3,384]{2,0,1:T(8,128)}, f32[384,768]{1,0:T(8,128)}, f32[768,1536]{1,0:T(8,128)}, ...) | async-done | bytes 14155792 | tf_op jit(solution)/shard_map/psum | solution.py:332
  (319 shorter events, 147.2 us)
Async XLA Ops:
  7.2 153.6 %copy-start = (bf16[768,1536]{1,0:T(8,128)(2,1)S(1)}, bf16[768,1536]{1,0:T(8,128)(2,1)}, u32[]{:S(2)}) copy-start(bf16[768,1536]{1,0:T(8,128)(2,1)} %param.45) | copy-start | bytes 7077892
  7.2 21.4 %all-gather.5.cloned.1.call-start = ((), (), s32[]{:S(2)}) async-start(), calls=%async_computation.5 | async-start | bytes 4718592 | tf_op jit(solution)/shard_map/all_gather | solution.py:264
  13.7 127.4 %reduce-scatter.6.cloned.1.call-start = ((), (), s32[]{:S(2)}) async-start(), calls=%async_computation.6 | async-start | bytes 9437184 | tf_op jit(solution)/shard_map/reduce_scatter | solution.py:277
  21.7 54.1 %copy-start.18 = (pred[512,512]{0,1:T(8,128)(4,1)}, pred[512,512]{0,1:T(8,128)(4,1)S(1)}, u32[]{:S(2)}) copy-start(pred[512,512]{0,1:T(8,128)(4,1)S(1)} %iota_compare_fusion.1) | copy-start | bytes 786436
  25.9 67.4 %copy-start.7 = (pred[512,1024]{1,0:T(8,128)(4,1)}, pred[512,1024]{1,0:T(8,128)(4,1)S(1)}, u32[]{:S(2)}) copy-start(pred[512,1024]{1,0:T(8,128)(4,1)S(1)} %iota_compare_fusion) | copy-start | bytes 1572868
  45.7 56.3 %copy-start.34 = (f32[6,1,2,1024]{3,1,2,0:T(1,128)}, f32[6,1,2,1024]{3,1,2,0:T(1,128)S(1)}, u32[]{:S(2)}) copy-start(f32[6,1,2,1024]{3,1,2,0:T(1,128)S(1)} %fusion.29) | copy-start | bytes 147460
  50.0 51.9 %copy-start.36 = (f32[6,1,2,1024]{3,1,2,0:T(1,128)}, f32[6,1,2,1024]{3,1,2,0:T(1,128)S(1)}, u32[]{:S(2)}) copy-start(f32[6,1,2,1024]{3,1,2,0:T(1,128)S(1)} %fusion.31) | copy-start | bytes 147460
  68.1 25.2 %copy-start.16 = (bf16[2,1024,6,64]{1,3,2,0:T(8,128)(2,1)}, bf16[2,1024,6,64]{1,3,2,0:T(8,128)(2,1)S(1)}, u32[]{:S(2)}) copy-start(bf16[2,1024,6,64]{1,3,2,0:T(8,128)(2,1)S(1)} %add_convert_fusion.4) | copy-start | bytes 4718596
  125.2 35.6 %all-gather.7.cloned.1.call-start = ((), (), s32[]{:S(2)}) async-start(), calls=%async_computation.7 | async-start | bytes 4718592 | tf_op jit(solution)/shard_map/all_gather | solution.py:280
  144.0 79.1 %copy-start.44 = (f32[2,512]{1,0:T(2,128)}, f32[2,512]{1,0:T(2,128)S(1)}, u32[]{:S(2)}) copy-start(f32[2,512]{1,0:T(2,128)S(1)} %broadcast_multiply_fusion.6) | copy-start | bytes 12292
  145.6 77.4 %copy-start.48 = (f32[2,512]{1,0:T(2,128)}, f32[2,512]{1,0:T(2,128)S(1)}, u32[]{:S(2)}) copy-start(f32[2,512]{1,0:T(2,128)S(1)} %add_rsqrt_fusion) | copy-start | bytes 12292
  147.3 28.2 %all-gather.9.cloned.1.call-start = ((), (), s32[]{:S(2)}) async-start(), calls=%async_computation.9 | async-start | bytes 4718592 | tf_op jit(solution)/shard_map/all_gather | solution.py:288
  147.9 70.4 %reduce-scatter.10.cloned.1.call-start = ((), (), s32[]{:S(2)}) async-start(), calls=%async_computation.10 | async-start | bytes 9437184 | tf_op jit(solution)/shard_map/reduce_scatter | solution.py:292
  202.5 20.6 %copy-start.14 = (bf16[2,512,768]{2,1,0:T(8,128)(2,1)S(1)}, bf16[2,512,768]{2,1,0:T(8,128)(2,1)}, u32[]{:S(2)}) copy-start(bf16[2,512,768]{2,1,0:T(8,128)(2,1)} %param.49) | copy-start | bytes 4718596
  202.5 38.3 %all-gather.11.cloned.1.call-start = ((), (), s32[]{:S(2)}) async-start(), calls=%async_computation.11 | async-start | bytes 4718592 | tf_op jit(solution)/shard_map/all_gather | solution.py:300
  227.4 315.4 %reduce-scatter.14.cloned.1.call-start = ((), (), s32[]{:S(2)}) async-start(), calls=%async_computation.13 | async-start | bytes 1179648 | tf_op jit(solution)/shard_map/reduce_scatter | solution.py:316
  244.3 28.1 %copy-start.32 = (bf16[2,1024,384]{1,2,0:T(8,128)(2,1)}, bf16[2,1024,384]{1,2,0:T(8,128)(2,1)S(1)}, u32[]{:S(2)}) copy-start(bf16[2,1024,384]{1,2,0:T(8,128)(2,1)S(1)} %convolution_convert_fusion) | copy-start | bytes 4718596
  288.3 73.9 %copy-start.42 = (f32[6,2,1024]{2,0,1:T(8,128)}, f32[6,2,1024]{2,0,1:T(8,128)S(1)}, u32[]{:S(2)}) copy-start(f32[6,2,1024]{2,0,1:T(8,128)S(1)} %get-tuple-element.174) | copy-start | bytes 147460
  297.9 246.8 %reduce-scatter.12.cloned.1.call-start = ((), (), s32[]{:S(2)}) async-start(), calls=%async_computation.12 | async-start | bytes 4718592 | tf_op jit(solution)/shard_map/reduce_scatter | solution.py:313
  332.1 21.4 %copy-start.13 = (bf16[2,1024,1,384]{1,3,2,0:T(8,128)(2,1)S(1)}, bf16[2,1024,1,384]{1,3,2,0:T(8,128)(2,1)}, u32[]{:S(2)}) copy-start(bf16[2,1024,1,384]{1,3,2,0:T(8,128)(2,1)} %slice.267) | copy-start | bytes 4718596
  390.2 157.4 %reduce-scatter.8.cloned.1.call-start = ((), (), s32[]{:S(2)}) async-start(), calls=%async_computation.8 | async-start | bytes 4718592 | tf_op jit(solution)/shard_map/reduce_scatter | solution.py:284
  399.3 433.3 %all-reduce.11.cloned.1.call-start = ((), (), s32[]{:S(2)}) async-start(), calls=%async_computation.14 | async-start | bytes 28311552 | tf_op jit(solution)/shard_map/psum | solution.py:332
  459.8 84.9 %copy-start.5 = (bf16[2,512,768]{2,1,0:T(8,128)(2,1)S(1)}, bf16[2,512,768]{2,1,0:T(8,128)(2,1)}, u32[]{:S(2)}) copy-start(bf16[2,512,768]{2,1,0:T(8,128)(2,1)} %param.32) | copy-start | bytes 4718596
  459.8 84.9 %copy-start.47 = (f32[2,512]{1,0:T(2,128)S(1)}, f32[2,512]{1,0:T(2,128)}, u32[]{:S(2)}) copy-start(f32[2,512]{1,0:T(2,128)} %copy-done.46) | copy-start | bytes 12292
  459.8 84.9 %copy-start.51 = (f32[2,512]{1,0:T(2,128)S(1)}, f32[2,512]{1,0:T(2,128)}, u32[]{:S(2)}) copy-start(f32[2,512]{1,0:T(2,128)} %copy-done.50) | copy-start | bytes 12292
  459.9 84.9 %copy-start.62 = (f32[768]{0:T(1024)S(1)}, f32[768]{0:T(1024)}, u32[]{:S(2)}) copy-start(f32[768]{0:T(1024)} %param.35) | copy-start | bytes 9220
  459.9 87.7 %copy-start.45 = (f32[2,512]{1,0:T(2,128)S(1)}, f32[2,512]{1,0:T(2,128)}, u32[]{:S(2)}) copy-start(f32[2,512]{1,0:T(2,128)} %copy-done.44) | copy-start | bytes 12292
  459.9 87.7 %copy-start.49 = (f32[2,512]{1,0:T(2,128)S(1)}, f32[2,512]{1,0:T(2,128)}, u32[]{:S(2)}) copy-start(f32[2,512]{1,0:T(2,128)} %copy-done.48) | copy-start | bytes 12292
  459.9 87.7 %copy-start.60 = (f32[768]{0:T(1024)S(1)}, f32[768]{0:T(1024)}, u32[]{:S(2)}) copy-start(f32[768]{0:T(1024)} %param.43) | copy-start | bytes 9220
  459.9 87.7 %copy-start.64 = (f32[2,512]{1,0:T(2,128)S(1)}, f32[2,512]{1,0:T(2,128)}, u32[]{:S(2)}) copy-start(f32[2,512]{1,0:T(2,128)} %copy-done.63) | copy-start | bytes 12292
  459.9 87.7 %copy-start.66 = (f32[2,512]{1,0:T(2,128)S(1)}, f32[2,512]{1,0:T(2,128)}, u32[]{:S(2)}) copy-start(f32[2,512]{1,0:T(2,128)} %copy-done.65) | copy-start | bytes 12292
  459.9 87.7 %copy-start.81 = (f32[768]{0:T(1024)S(1)}, f32[768]{0:T(1024)}, u32[]{:S(2)}) copy-start(f32[768]{0:T(1024)} %param.48) | copy-start | bytes 9220
  (83 other events, 626.7 us)
Sparse Core Ops, SparseCore 0:
  13.8 14.8 all-gather.4
  125.3 15.6 reduce-scatter.5
  147.5 13.2 all-gather.6
  162.3 13.2 all-gather.8
  202.6 15.6 reduce-scatter.9
  227.5 13.2 all-gather.10
  298.0 9.4 reduce-scatter.13
  390.3 12.0 reduce-scatter.11
  404.7 12.0 reduce-scatter.7
  431.3 401.2 all-reduce.10
where the time goes:
time: 861 us; the launch traced here: 851 us
  waiting for transfers between devices  299 us (35%)
  matrix products  290 us (34%)
  blocking collectives  125 us (15%)
  other arithmetic  83.4 us (10%)
  local copies, waits for them, and re-layouts  37.8 us (4%)
  between operations  15.9 us (2%)
    dot_general x33, matrix products, matrix_multiply(): jnp.einsum(form, left_side, right_side, preferred_element_type=jnp.float32)  254 us
    psum x1, waiting for transfers between devices, per_device(): lax.psum((qkv_grad, qv_grad, memw_grad, memb_grad, outw_grad, up_output_g...  236 us
    psum x1, blocking collectives, per_device(): lax.psum((qkv_grad, qv_grad, memw_grad, memb_grad, outw_grad, up_output_g...  81.6 us
    psum x1, blocking collectives, per_device(): lax.psum((first_gain_grad, first_bias_grad, out_bias_grad, second_gain_gr...  40.4 us
    dot_general x4, matrix products, product(): jnp.einsum(form, left_side, right_side, precision=lax.Precision.HIGHEST)  35.6 us
    convert_element_type x2, other arithmetic, attend_backward(): (weights * (weights_grad - inner_sum)).astype(jnp.bfloat16)  28.5 us
    unnamed x215, local copies, waits for them, and re-layouts  21.9 us
  transfers between devices with their start and end apart: 10, of which 7 were waited for; matrix products, arithmetic and copies ran while one was open for 23% of the time, Pallas kernels for 0%

commit v1 on v0

--- a/solution.py
+++ b/solution.py
@@ -342,6 +342,7 @@
         ),
         "batch",
     )
+    packet_pair = lambda t0: lax.psum(lax.psum(t0, axis_name="batch"), "mp")
     (
         first_gain_grad,
         first_bias_grad,
@@ -349,7 +350,7 @@
         second_gain_grad,
         second_bias_grad,
         down_bias_grad,
-    ) = lax.psum(
+    ) = packet_pair(
         (
             first_gain_grad,
             first_bias_grad,
@@ -357,8 +358,7 @@
             second_gain_grad,
             second_bias_grad,
             down_bias_grad,
-        ),
-        ("batch", "mp"),
+        )
     )
     return (
         block_out,

time: 861 us -> 859 us (level)
  blocking collectives: 125 us -> 88.9 us
  waiting for transfers between devices: 299 us -> 333 us
    psum x2, blocking collectives: 122 us -> 86.5 us  [per_device(): packet_pair = lambda t0: lax.psum(lax.psum(t0, axis_name='batch'), 'mp')]
    psum x1, waiting for transfers between devices: 236 us -> 270 us  [per_device(): lax.psum((qkv_grad, qv_grad, memw_grad, memb_grad, outw_grad, up_output_g...]
where the time goes in v1:
time: 859 us; the launch traced here: 849 us
  waiting for transfers between devices  333 us (39%)
  matrix products  290 us (34%)
  blocking collectives  88.9 us (10%)
  other arithmetic  83.3 us (10%)
  local copies, waits for them, and re-layouts  37.7 us (4%)
  between operations  15.8 us (2%)
    psum x1, waiting for transfers between devices, per_device(): lax.psum((qkv_grad, qv_grad, memw_grad, memb_grad, outw_grad, up_output_g...  270 us
    dot_general x33, matrix products, matrix_multiply(): jnp.einsum(form, left_side, right_side, preferred_element_type=jnp.float32)  254 us
    psum x2, blocking collectives, per_device(): packet_pair = lambda t0: lax.psum(lax.psum(t0, axis_name='batch'), 'mp')  86.5 us
    dot_general x4, matrix products, product(): jnp.einsum(form, left_side, right_side, precision=lax.Precision.HIGHEST)  35.6 us
    convert_element_type x2, other arithmetic, attend_backward(): (weights * (weights_grad - inner_sum)).astype(jnp.bfloat16)  28.5 us
    unnamed x215, local copies, waits for them, and re-layouts  21.8 us
  transfers between devices with their start and end apart: 10, of which 7 were waited for; matrix products, arithmetic and copies ran while one was open for 23% of the time, Pallas kernels for 0%

profile of v1, /device:TPU:0, one launch (start us, length us, event | category | flops | bytes accessed | tf_op | source)
XLA Modules:
  0.0 849.1 jit_solution(3796491954438523466)
XLA Ops:
  50.0 7.1 fusion.54
  57.1 10.7 %fusion.34 = (f32[2,6,512]{2,1,0:T(8,128)S(1)}, f32[2,6,512,1024]{3,2,1,0:T(8,128)}) fusion(pred[512,1024]{1,0:T(8,128)(4,1)S(1)} %iota_compare_fusion, bf16[2,1024,6,64]{1,3,2,0:T(8,128)(2,1)S(1)} %bitcast.292, bf16[2,1024,6,64]{1,3,2,0:T(8,128)(2,1)S(1)} %add_convert_fusion.3), kind=kOutput, calls=%fused_computation.57 | convolution fusion | flops 824174592 | bytes 28073984 | tf_op jit(solution)/shard_map/sqhd,skhd->shqk/dot_general | solution.py:15
  68.1 7.7 fusion.24
  75.9 7.7 fusion.98
  85.9 7.3 fusion
  93.3 8.5 %fusion.102 = f32[2,512,6,64]{1,3,2,0:T(8,128)} fusion(bf16[2,1024,6,64]{1,3,2,0:T(8,128)(2,1)S(1)} %add_convert_fusion.4, f32[2,6,512]{2,1,0:T(8,128)S(1)} %fusion, f32[2,6,512]{2,1,0:T(8,128)S(1)} %get-tuple-element.170, f32[2,6,512,1024]{3,2,1,0:T(8,128)S(1)} %bitcast.288, pred[512,1024]{1,0:T(8,128)(4,1)S(1)} %iota_compare_fusion), kind=kOutput, calls=%fused_computation.147 | convolution fusion | flops 836763648 | bytes 28884992 | tf_op jit(solution)/shard_map/shqk,skhd->sqhd/dot_general | solution.py:15
  102.8 16.8 %fusion.70 = bf16[2,1024,6,64]{1,3,2,0:T(8,128)(2,1)S(1)} fusion(f32[2,512,6,64]{1,3,2,0:T(8,128)} %fusion.102, f32[2,512,6,64]{1,3,2,0:T(8,128)} %fusion.98, bf16[2,256,6,64]{1,3,2,0:T(8,128)(2,1)S(1)} %bitcast.314, f32[2,1024,6]{1,2,0:T(8,128)S(1)} %get-tuple-element.155, f32[2,1024,6]{1,2,0:T(8,128)S(1)} %get-tuple-element.157, ...), kind=kOutput, calls=%fused_computation.105 | convolution fusion | flops 427819008 | bytes 5260296 | tf_op jit(solution)/shard_map/slhn,snhd->slhd/dot_general | solution.py:15
  125.3 15.8 %reduce-scatter.6.cloned.1.call-done = f32[2,512,768]{2,1,0:T(8,128)} async-done(((f32[2,1024,768]{2,1,0:T(8,128)}), f32[2,512,768]{2,1,0:T(8,128)}) %reduce-scatter.6.cloned.1.call-update) | async-done | bytes 3145744 | tf_op jit(solution)/shard_map/reduce_scatter | solution.py:277
  148.0 12.8 %all-gather.7.cloned.1.call-done = bf16[2,1024,768]{2,1,0:T(8,128)(2,1)} async-done(((bf16[2,512,768]{2,1,0:T(8,128)(2,1)}), bf16[2,1024,768]{2,1,0:T(8,128)(2,1)}) %all-gather.7.cloned.1.call-update) | async-done | bytes 3145744 | tf_op jit(solution)/shard_map/all_gather | solution.py:280
  160.8 13.4 %multiply_convert_fusion.2 = (bf16[2,1024,1536]{2,1,0:T(8,128)(2,1)}, f32[2,1024,1536]{2,1,0:T(8,128)}) fusion(f32[1536]{0:T(1024)S(1)} %convert_element_type.137, bf16[2,1024,768]{2,1,0:T(8,128)(2,1)} %all-gather.7.cloned.1.call-done, bf16[768,1536]{1,0:T(8,128)(2,1)S(1)} %copy-done), kind=kOutput, calls=%fused_computation.40 | convolution fusion | flops 4863295488 | bytes 24385536 | tf_op jit(solution)/shard_map/ahg,gm->ahm/dot_general | solution.py:15
  175.6 17.3 %convert_reduce_fusion = (f32[1536]{0:T(1024)}, bf16[2,1024,1536]{2,1,0:T(8,128)(2,1)S(1)}) fusion(f32[2,1024,1536]{2,1,0:T(8,128)} %get-tuple-element.177, f32[1536]{0:T(1024)S(1)} %convert_element_type.137, bf16[2,1024,768]{2,1,0:T(8,128)(2,1)} %all-gather.9.cloned.1.call-done, bf16[1536,768]{1,0:T(8,128)(2,1)} %param.47), kind=kOutput, calls=%fused_computation.34 | convolution fusion | flops 4904188416 | bytes 24391680 | tf_op jit(solution)/shard_map/kpo,wo->kpw/dot_general | solution.py:15
  195.6 6.9 fusion.82
  202.5 15.8 %reduce-scatter.10.cloned.1.call-done = f32[2,512,768]{2,1,0:T(8,128)} async-done(((f32[2,1024,768]{2,1,0:T(8,128)}), f32[2,512,768]{2,1,0:T(8,128)}) %reduce-scatter.10.cloned.1.call-update) | async-done | bytes 3145744 | tf_op jit(solution)/shard_map/reduce_scatter | solution.py:292
  227.5 13.3 %all-gather.11.cloned.1.call-done = bf16[2,1024,768]{2,1,0:T(8,128)(2,1)} async-done(((bf16[2,512,768]{2,1,0:T(8,128)(2,1)}), bf16[2,1024,768]{2,1,0:T(8,128)(2,1)}) %all-gather.11.cloned.1.call-update) | async-done | bytes 3145744 | tf_op jit(solution)/shard_map/all_gather | solution.py:300
  244.3 8.0 fusion.99
  252.8 6.9 multiply_reduce_fusion.1
  259.6 7.1 multiply_convert_fusion.1
  276.7 11.3 %fusion.6 = (f32[2,1024,6]{1,2,0:T(8,128)S(1)}, f32[2,1024,6]{1,2,0:T(8,128)S(1)}, f32[2,1024,6]{1,2,0:T(8,128)S(1)}) fusion(f32[2,1024,6]{1,2,0:T(8,128)S(1)} %copy-done.52, f32[2,1024,6]{1,2,0:T(8,128)S(1)} %copy-done.58, f32[256]{0:T(256)S(1)} %copy-done.90, f32[2,1024,6]{1,2,0:T(8,128)S(1)} %copy-done.54, f32[2,1024,6]{1,2,0:T(8,128)S(1)} %get-tuple-element.154, ...), kind=kOutput, calls=%fused_computation.17 | convolution fusion | flops 460025856 | bytes 2311172 | tf_op jit(solution)/shard_map/slhd,snhd->slhn/dot_general | solution.py:15
  298.0 18.1 %multiply_reduce_fusion = (f32[2,6,512]{2,1,0:T(8,128)S(1)}, f32[2,6,512,1024]{3,2,1,0:T(8,128)}) fusion(f32[2,6,512]{2,1,0:T(8,128)S(1)} %log_add_fusion, f32[2,6,512,1024]{3,2,1,0:T(8,128)} %get-tuple-element.171, pred[512,1024]{1,0:T(8,128)(4,1)S(1)} %copy-done.8, bf16[2,1024,6,64]{1,3,2,0:T(8,128)(2,1)} %copy-done.16, bf16[2,1024,6,64]{1,3,2,0:T(8,128)(2,1)} %bitcast.312), kind=kOutput, calls=%fused_computation.1 | convolution fusion | flops 836757504 | bytes 53264384 | tf_op jit(solution)/shard_map/sqhd,skhd->shqk/dot_general | solution.py:15
  316.1 13.5 %fusion.76 = bf16[2,1024,6,64]{1,3,2,0:T(8,128)(2,1)} fusion(f32[2,512,6,64]{1,3,2,0:T(8,128)} %fusion.99, f32[2,6,512]{2,1,0:T(8,128)S(1)} %log_add_fusion, f32[2,6,512,1024]{3,2,1,0:T(8,128)} %get-tuple-element.171, pred[512,1024]{1,0:T(8,128)(4,1)S(1)} %copy-done.8, bf16[2,1024,6,64]{1,3,2,0:T(8,128)(2,1)} %bitcast.313), kind=kOutput, calls=%fused_computation.113 | convolution fusion | flops 832045056 | bytes 29646848 | tf_op jit(solution)/shard_map/shqk,sqhd->skhd/dot_general | solution.py:15
  332.1 21.4 %multiply_convert_fusion = bf16[2,6,512,1024]{3,2,1,0:T(8,128)(2,1)} fusion(f32[2,6,512,1024]{3,2,1,0:T(8,128)} %get-tuple-element.175, f32[2,6,512]{2,1,0:T(8,128)S(1)} %get-tuple-element.174, f32[2,6,512]{2,1,0:T(8,128)S(1)} %log_add_fusion, f32[2,6,512,1024]{3,2,1,0:T(8,128)} %get-tuple-element.171, pred[512,1024]{1,0:T(8,128)(4,1)S(1)} %copy-done.8), kind=kLoop, calls=%fused_computation | loop fusion | flops 37748736 | bytes 63488000 | tf_op jit(solution)/shard_map/convert_element_type | solution.py:178
  353.5 8.6 %multiply_bitcast_fusion.2 = f32[2,512,6,64]{1,3,2,0:T(8,128)S(1)} fusion(bf16[2,1024,6,64]{1,3,2,0:T(8,128)(2,1)S(1)} %bitcast.294, bf16[2,6,512,1024]{3,2,1,0:T(8,128)(2,1)} %multiply_convert_fusion), kind=kOutput, calls=%fused_computation.143 | convolution fusion | flops 805699584 | bytes 15728640 | tf_op jit(solution)/shard_map/shqk,skhd->sqhd/dot_general | solution.py:15
  370.6 8.4 fusion.77
  381.8 8.4 bitcast_convert_fusion
  390.3 9.0 %fusion.86 = bf16[2,1024,768]{2,1,0:T(8,128)(2,1)} fusion(bf16[2,1024,1536]{2,1,0:T(8,128)(2,1)} %get-tuple-element.176, bf16[1536,768]{1,0:T(8,128)(2,1)} %param.47), kind=kOutput, calls=%fused_computation.135 | convolution fusion | flops 4833411072 | bytes 11796480 | tf_op jit(solution)/shard_map/hom,mu->hou/dot_general | solution.py:15
  399.4 10.4 %convolution_bitcast_fusion.1 = f32[768,1536]{1,0:T(8,128)} fusion(bf16[2,1024,768]{2,1,0:T(8,128)(2,1)} %all-gather.7.cloned.1.call-done, bf16[2,1024,1536]{2,1,0:T(8,128)(2,1)} %copy-done.91), kind=kOutput, calls=%fused_computation.90 | convolution fusion | flops 4831838208 | bytes 14155776 | tf_op jit(solution)/shard_map/orx,ora->xa/dot_general | solution.py:15
  409.7 8.9 %convolution_bitcast_fusion = f32[1536,768]{1,0:T(8,128)} fusion(bf16[2,1024,1536]{2,1,0:T(8,128)(2,1)} %get-tuple-element.176, bf16[2,1024,768]{2,1,0:T(8,128)(2,1)S(1)} %copy-done.85), kind=kOutput, calls=%fused_computation.89 | convolution fusion | flops 4831838208 | bytes 14155776 | tf_op jit(solution)/shard_map/qro,qrv->ov/dot_general | solution.py:15
  432.0 13.3 %fusion.27 = f32[6,1,256,1]{2,1,3,0:T(1,128)S(1)} fusion(f32[2,1024,6,256]{1,3,2,0:T(8,128)} %copy-done.2, f32[6,2,1024,1]{2,0,1,3:T(8,128)S(1)} %bitcast.319), kind=kOutput, calls=%fused_computation.50 | convolution fusion | flops 37748736 | bytes 12638208 | tf_op jit(solution)/shard_map/transpose(jvp(slhn,hn->slh))/dot_general | solution.py:11
  445.4 13.4 %fusion.25 = f32[6,1,256,1]{2,1,3,0:T(1,128)S(1)} fusion(f32[2,1024,6,256]{1,3,2,0:T(8,128)} %copy-done.2, f32[6,2,1024,1]{2,0,1,3:T(8,128)S(1)} %bitcast.318), kind=kOutput, calls=%fused_computation.48 | convolution fusion | flops 37748736 | bytes 12638208 | tf_op jit(solution)/shard_map/transpose(jvp(slhn,hn->slh))/dot_general | solution.py:11
  465.3 8.3 fusion.66
  473.6 82.5 %all-reduce.6 = (f32[768]{0:T(1024)S(1)}, f32[768]{0:T(1024)S(1)}, f32[2,384]{1,0:T(2,128)}, f32[2,6,256]{2,1,0:T(8,128)S(1)}, f32[2,6]{1,0:T(2,128)}, /*index=5...) all-reduce(f32[768]{0:T(1024)S(1)} %get-tuple-element.115, ...), channel_id=1, replica_groups=mesh['batch'=16,'mp'=2] {'batch'}, use_global_device_ids=true, to_apply=%region_23.24 | all-reduce | flops 9996 | bytes 79968 | tf_op jit(solution)/shard_map/psum | solution.py:345
  560.7 270.3 %all-reduce.11.cloned.1.call-done = (f32[768,3,384]{2,0,1:T(8,128)}, f32[384,768]{1,0:T(8,128)}, f32[768,1536]{1,0:T(8,128)}, f32[1536,768]{1,0:T(8,128)}) async-done(((f32[768,3,384]{2,0,1:T(8,128)}, f32[384,768]{1,0:T(8,128)}, f32[768,1536]{1,0:T(8,128)}, f32[1536,768]{1,0:T(8,128)}), (f32[768,3,384]{2,0,1:T(8,128)}, f32[384,768]{1,0:T(8,128)}, f32[768,1536]{1,0:T(8,128)}, ...) | async-done | bytes 14155792 | tf_op jit(solution)/shard_map/psum | solution.py:332
  (319 shorter events, 144.3 us)
Async XLA Ops:
  7.2 153.6 %copy-start = (bf16[768,1536]{1,0:T(8,128)(2,1)S(1)}, bf16[768,1536]{1,0:T(8,128)(2,1)}, u32[]{:S(2)}) copy-start(bf16[768,1536]{1,0:T(8,128)(2,1)} %param.45) | copy-start | bytes 7077892
  7.2 21.4 %all-gather.5.cloned.1.call-start = ((), (), s32[]{:S(2)}) async-start(), calls=%async_computation.5 | async-start | bytes 4718592 | tf_op jit(solution)/shard_map/all_gather | solution.py:264
  13.7 127.4 %reduce-scatter.6.cloned.1.call-start = ((), (), s32[]{:S(2)}) async-start(), calls=%async_computation.6 | async-start | bytes 9437184 | tf_op jit(solution)/shard_map/reduce_scatter | solution.py:277
  20.1 19.1 %copy-start.30 = (bf16[2,256,1,384]{1,3,0,2:T(8,128)(2,1)}, bf16[2,256,1,384]{1,3,0,2:T(8,128)(2,1)S(1)}, u32[]{:S(2)}) copy-start(bf16[2,256,1,384]{1,3,0,2:T(8,128)(2,1)S(1)} %copy.61) | copy-start | bytes 1179652
  21.7 54.1 %copy-start.18 = (pred[512,512]{0,1:T(8,128)(4,1)}, pred[512,512]{0,1:T(8,128)(4,1)S(1)}, u32[]{:S(2)}) copy-start(pred[512,512]{0,1:T(8,128)(4,1)S(1)} %iota_compare_fusion.1) | copy-start | bytes 786436
  25.9 67.4 %copy-start.7 = (pred[512,1024]{1,0:T(8,128)(4,1)}, pred[512,1024]{1,0:T(8,128)(4,1)S(1)}, u32[]{:S(2)}) copy-start(pred[512,1024]{1,0:T(8,128)(4,1)S(1)} %iota_compare_fusion) | copy-start | bytes 1572868
  39.3 17.9 %copy-start.9 = (bf16[2,1024,6,64]{1,3,2,0:T(8,128)(2,1)}, bf16[2,1024,6,64]{1,3,2,0:T(8,128)(2,1)S(1)}, u32[]{:S(2)}) copy-start(bf16[2,1024,6,64]{1,3,2,0:T(8,128)(2,1)S(1)} %add_convert_fusion.3) | copy-start | bytes 4718596
  45.7 56.3 %copy-start.34 = (f32[6,1,2,1024]{3,1,2,0:T(1,128)}, f32[6,1,2,1024]{3,1,2,0:T(1,128)S(1)}, u32[]{:S(2)}) copy-start(f32[6,1,2,1024]{3,1,2,0:T(1,128)S(1)} %fusion.29) | copy-start | bytes 147460
  50.0 51.9 %copy-start.36 = (f32[6,1,2,1024]{3,1,2,0:T(1,128)}, f32[6,1,2,1024]{3,1,2,0:T(1,128)S(1)}, u32[]{:S(2)}) copy-start(f32[6,1,2,1024]{3,1,2,0:T(1,128)S(1)} %fusion.31) | copy-start | bytes 147460
  68.1 25.2 %copy-start.16 = (bf16[2,1024,6,64]{1,3,2,0:T(8,128)(2,1)}, bf16[2,1024,6,64]{1,3,2,0:T(8,128)(2,1)S(1)}, u32[]{:S(2)}) copy-start(bf16[2,1024,6,64]{1,3,2,0:T(8,128)(2,1)S(1)} %add_convert_fusion.4) | copy-start | bytes 4718596
  68.1 15.5 %slice-start = ((s8[25165824]{0:T(1024)(128)(4,1)}), s8[4194304]{0:T(1024)(128)(4,1)S(1)}, s32[]{:S(2)}) async-start(s8[25165824]{0:T(1024)(128)(4,1)} %bitcast.287), calls=%async_computation.15 | async-start | bytes 8388608
  68.1 15.5 %slice-start.1 = ((s8[25165824]{0:T(1024)(128)(4,1)}), s8[4194304]{0:T(1024)(128)(4,1)S(1)}, s32[]{:S(2)}) async-start(s8[25165824]{0:T(1024)(128)(4,1)} %bitcast.287), calls=%async_computation.16 | async-start | bytes 8388608
  102.0 17.6 %copy-start.57 = (f32[2,1024,6]{1,2,0:T(8,128)}, f32[2,1024,6]{1,2,0:T(8,128)S(1)}, u32[]{:S(2)}) copy-start(f32[2,1024,6]{1,2,0:T(8,128)S(1)} %fusion.189) | copy-start | bytes 147460
  102.8 16.8 %copy-start.53 = (f32[2,1024,6]{1,2,0:T(8,128)}, f32[2,1024,6]{1,2,0:T(8,128)S(1)}, u32[]{:S(2)}) copy-start(f32[2,1024,6]{1,2,0:T(8,128)S(1)} %get-tuple-element.157) | copy-start | bytes 147460
  102.8 16.8 %copy-start.55 = (f32[2,1024,6]{1,2,0:T(8,128)}, f32[2,1024,6]{1,2,0:T(8,128)S(1)}, u32[]{:S(2)}) copy-start(f32[2,1024,6]{1,2,0:T(8,128)S(1)} %get-tuple-element.155) | copy-start | bytes 147460
  102.8 18.0 %copy-start.38 = (bf16[384,768]{1,0:T(8,128)(2,1)S(1)}, bf16[384,768]{1,0:T(8,128)(2,1)}, u32[]{:S(2)}) copy-start(bf16[384,768]{1,0:T(8,128)(2,1)} %param.41) | copy-start | bytes 1769476
  125.2 15.9 %copy-start.79 = (f32[768]{0:T(1024)S(1)}, f32[768]{0:T(1024)}, u32[]{:S(2)}) copy-start(f32[768]{0:T(1024)} %param.42) | copy-start | bytes 9220
  125.2 35.6 %all-gather.7.cloned.1.call-start = ((), (), s32[]{:S(2)}) async-start(), calls=%async_computation.7 | async-start | bytes 4718592 | tf_op jit(solution)/shard_map/all_gather | solution.py:280
  144.0 79.1 %copy-start.44 = (f32[2,512]{1,0:T(2,128)}, f32[2,512]{1,0:T(2,128)S(1)}, u32[]{:S(2)}) copy-start(f32[2,512]{1,0:T(2,128)S(1)} %broadcast_multiply_fusion.6) | copy-start | bytes 12292
  145.6 77.4 %copy-start.48 = (f32[2,512]{1,0:T(2,128)}, f32[2,512]{1,0:T(2,128)S(1)}, u32[]{:S(2)}) copy-start(f32[2,512]{1,0:T(2,128)S(1)} %add_rsqrt_fusion) | copy-start | bytes 12292
  147.3 28.2 %all-gather.9.cloned.1.call-start = ((), (), s32[]{:S(2)}) async-start(), calls=%async_computation.9 | async-start | bytes 4718592 | tf_op jit(solution)/shard_map/all_gather | solution.py:288
  147.9 70.4 %reduce-scatter.10.cloned.1.call-start = ((), (), s32[]{:S(2)}) async-start(), calls=%async_computation.10 | async-start | bytes 9437184 | tf_op jit(solution)/shard_map/reduce_scatter | solution.py:292
  202.5 20.6 %copy-start.14 = (bf16[2,512,768]{2,1,0:T(8,128)(2,1)S(1)}, bf16[2,512,768]{2,1,0:T(8,128)(2,1)}, u32[]{:S(2)}) copy-start(bf16[2,512,768]{2,1,0:T(8,128)(2,1)} %param.49) | copy-start | bytes 4718596
  202.5 38.3 %all-gather.11.cloned.1.call-start = ((), (), s32[]{:S(2)}) async-start(), calls=%async_computation.11 | async-start | bytes 4718592 | tf_op jit(solution)/shard_map/all_gather | solution.py:300
  227.4 233.1 %reduce-scatter.14.cloned.1.call-start = ((), (), s32[]{:S(2)}) async-start(), calls=%async_computation.13 | async-start | bytes 1179648 | tf_op jit(solution)/shard_map/reduce_scatter | solution.py:316
  227.5 16.8 %copy-start.19 = (pred[512,512]{0,1:T(8,128)(4,1)S(1)}, pred[512,512]{0,1:T(8,128)(4,1)}, u32[]{:S(2)}) copy-start(pred[512,512]{0,1:T(8,128)(4,1)} %copy-done.18) | copy-start | bytes 786436
  244.3 28.1 %copy-start.32 = (bf16[2,1024,384]{1,2,0:T(8,128)(2,1)}, bf16[2,1024,384]{1,2,0:T(8,128)(2,1)S(1)}, u32[]{:S(2)}) copy-start(bf16[2,1024,384]{1,2,0:T(8,128)(2,1)S(1)} %convolution_convert_fusion) | copy-start | bytes 4718596
  288.3 73.9 %copy-start.42 = (f32[6,2,1024]{2,0,1:T(8,128)}, f32[6,2,1024]{2,0,1:T(8,128)S(1)}, u32[]{:S(2)}) copy-start(f32[6,2,1024]{2,0,1:T(8,128)S(1)} %get-tuple-element.180) | copy-start | bytes 147460
  297.9 164.5 %reduce-scatter.12.cloned.1.call-start = ((), (), s32[]{:S(2)}) async-start(), calls=%async_computation.12 | async-start | bytes 4718592 | tf_op jit(solution)/shard_map/reduce_scatter | solution.py:313
  332.1 21.4 %copy-start.13 = (bf16[2,1024,1,384]{1,3,2,0:T(8,128)(2,1)S(1)}, bf16[2,1024,1,384]{1,3,2,0:T(8,128)(2,1)}, u32[]{:S(2)}) copy-start(bf16[2,1024,1,384]{1,3,2,0:T(8,128)(2,1)} %slice.267) | copy-start | bytes 4718596
  390.2 75.1 %reduce-scatter.8.cloned.1.call-start = ((), (), s32[]{:S(2)}) async-start(), calls=%async_computation.8 | async-start | bytes 4718592 | tf_op jit(solution)/shard_map/reduce_scatter | solution.py:284
  399.3 431.7 %all-reduce.11.cloned.1.call-start = ((), (), s32[]{:S(2)}) async-start(), calls=%async_computation.14 | async-start | bytes 28311552 | tf_op jit(solution)/shard_map/psum | solution.py:332
  (83 other events, 507.1 us)
Sparse Core Ops, SparseCore 0:
  13.8 14.8 all-gather.4
  125.3 15.6 reduce-scatter.5
  147.5 13.2 all-gather.6
  162.3 13.2 all-gather.8
  202.6 15.6 reduce-scatter.9
  227.5 13.2 all-gather.10
  298.0 9.4 reduce-scatter.13
  390.3 12.0 reduce-scatter.11
  404.7 12.0 reduce-scatter.7
  431.3 399.6 all-reduce.10
